TPU v7x, 256 devices: a whole 4x4x8 slice. The times are simulated.
256 devices in a mesh: ma: 32 (over z, y), freq: 8 (over x, core).
Axes of the slice: x: 4, y: 4, z: 8, core: 2. Of those that a mesh axis runs over, the one named last changes fastest.
Arguments:
- visibilities: bfloat16 [512, 32, 4, 512], P('ma', 'freq'), may hold values from -6 to 6
- transfer: bfloat16 [32, 64, 512, 1024], P('freq', 'ma'), may hold values from -1 to 1, as said below
- noise_weight: float32 [32, 512], P('freq'), may hold values from 1 to 12, as said below
- freq_prior: float32 [32, 32], P('freq'), may hold values from -1 to 5, as said below
Outputs:
- sky_map: float32 [32, 64, 4, 1024], P('freq', 'ma')
- residual: float32 [32, 64, 4, 1024], P('freq', 'ma')
- direction: float32 [32, 64, 4, 1024], P('freq', 'ma')
Inputs may be any that keep to these rules, and one draw needn't show every extreme that they name: Real transfer blocks of the m-modes in the window. `noise_weight`: positive weights. `freq_prior`: symmetric positive definite.
All inputs are finite; a program needn't handle non-finite values.
Results may differ from a plain program's by a relative error of at most 0.0056.
Values may be sent and summed in bfloat16 or wider, within the bound.
A program may use at most 64 MiB of HBM per device.

v0:
```python
import math
import jax
import jax.numpy as jnp
from jax import lax
from jax.sharding import PartitionSpec as P


def harmonic_lookup(harmonic_number, leading_epoch, epoch_number, whole_epoch_grid):
    harmonic_slot = jnp.arange(harmonic_number, dtype=jnp.int32)
    observing_epochs = leading_epoch + jnp.arange(epoch_number, dtype=jnp.int32)
    rotation_argument = harmonic_slot[:, None] * observing_epochs[None, :] % whole_epoch_grid
    rotation_radians = rotation_argument.astype(jnp.float32) * (2.0 * math.pi / whole_epoch_grid)
    return (
        (jnp.cos(rotation_radians) + jnp.sin(rotation_radians))
        * (1.0 / math.sqrt(whole_epoch_grid))
    ).astype(jnp.bfloat16)


def local(visibilities, transfer, noise_weight, freq_prior):
    epochs_each_shard, frequency_per_device, realization_count, baseline_pairs = visibilities.shape
    harmonics_each_shard = transfer.shape[1]
    harmonic_amount = lax.axis_size("ma")
    whole_epoch_grid = epochs_each_shard * harmonic_amount
    column_total = frequency_per_device * realization_count * baseline_pairs
    flat_vis = visibilities.reshape(epochs_each_shard, column_total)
    leading_epoch = lax.axis_index("ma") * epochs_each_shard
    cas_rows = harmonic_lookup(
        harmonics_each_shard * lax.axis_size("ma"),
        leading_epoch,
        epochs_each_shard,
        whole_epoch_grid,
    )
    mode_totals = lax.psum_scatter(
        jnp.dot(cas_rows, flat_vis, preferred_element_type=jnp.float32),
        "ma",
        scatter_dimension=0,
        tiled=True,
    )
    visibility_modes = mode_totals.reshape(
        harmonics_each_shard, frequency_per_device, realization_count, baseline_pairs
    )
    weighted = (noise_weight[None, :, None, :] * visibility_modes).astype(jnp.bfloat16)
    right_side = jnp.einsum(
        "fmbs,mfkb->fmks", transfer, weighted, preferred_element_type=jnp.float32
    )
    right_low = right_side.astype(jnp.bfloat16)
    observed = jnp.einsum(
        "fmbs,fmks->fmkb", transfer, right_low, preferred_element_type=jnp.float32
    )
    scaled = (noise_weight[:, None, None, :] * observed).astype(jnp.bfloat16)
    adjoint = jnp.einsum("fmbs,fmkb->fmks", transfer, scaled, preferred_element_type=jnp.float32)
    coupled = jnp.einsum(
        "fg,gmks->fmks",
        freq_prior,
        lax.all_gather(right_side, "freq", axis=0, tiled=True),
        precision=lax.Precision.HIGHEST,
    )
    applied = adjoint + coupled
    local_norm = jnp.sum(right_side * right_side, axis=(0, 1, 3))
    local_curve = jnp.sum(right_side * applied, axis=(0, 1, 3))
    norm_now = lax.psum(local_norm, ("ma", "freq"))
    curvature = lax.psum(local_curve, ("ma", "freq"))
    step_plain = norm_now / curvature
    residual = right_side - step_plain[None, None, :, None] * applied
    norm_next = lax.psum(jnp.sum(residual * residual, axis=(0, 1, 3)), ("ma", "freq"))
    sky_map = step_plain[None, None, :, None] * right_side
    direction = residual + (norm_next / norm_now)[None, None, :, None] * right_side
    return (sky_map, residual, direction)


def solution(mesh):
    return jax.shard_map(
        local,
        mesh=mesh,
        in_specs=(
            P("ma", "freq", None, None),
            P("freq", "ma", None, None),
            P("freq", None),
            P("freq", None),
        ),
        out_specs=(
            P("freq", "ma", None, None),
            P("freq", "ma", None, None),
            P("freq", "ma", None, None),
        ),
        check_vma=False,
    )
```

profile of v0, /device:TPU:1, one launch (start us, length us, event | category | flops | bytes accessed | tf_op | source)
XLA Modules:
  0.0 370.0 jit_solution(2050857011195431761)
XLA Ops:
  7.2 0.0 copy-start
  7.2 0.0 copy-start.2
  7.2 0.0 all-reduce.4.cloned.1.call-start
  7.2 1.1 reshape.20
  8.4 1.9 fusion.16
  10.3 0.0 all-reduce.4.cloned.1.call-update
  10.3 0.0 all-gather.2.cloned.1.call-start
  10.3 1.3 dynamic-slice
  12.3 153.0 %all-reduce.4.cloned.1.call-done = f32[64,8192]{1,0:T(8,128)} async-done(((f32[64,8192]{1,0:T(8,128)}), f32[64,8192]{1,0:T(8,128)}) %all-reduce.4.cloned.1.call-update) | async-done | bytes 2097168
  165.3 1.0 constant_dynamic-slice_fusion
  166.3 0.1 reshape.21
  166.3 5.3 %fusion.6 = f32[4,2,4,1024]{3,2,1,0:T(4,128)} fusion(bf16[4,2,512,1024]{3,2,1,0:T(8,128)(2,1)} %param.5, f32[2,4,4,512]{3,2,1,0:T(4,128)S(1)} %reshape.21, f32[4,512]{1,0:T(4,128)} %param.6), kind=kOutput, calls=%fused_computation.14 | convolution fusion | flops 33587200 | bytes 8593408 | tf_op jit(solution)/shard_map/fmbs,mfkb->fmks/dot_general | solution.py:43
  171.6 0.0 all-gather.2.cloned.1.call-update
  171.6 27.8 %all-gather.2.cloned.1.call-done = f32[32,2,4,1024]{3,2,1,0:T(4,128)} async-done(((f32[4,2,4,1024]{3,2,1,0:T(4,128)}), f32[32,2,4,1024]{3,2,1,0:T(4,128)}) %all-gather.2.cloned.1.call-update) | async-done | bytes 1048592 | tf_op jit(solution)/shard_map/all_gather | solution.py:55
  199.4 0.0 copy-done
  199.4 2.4 fusion.1
  201.8 0.0 copy-done.2
  201.8 0.0 copy-start.1
  201.8 9.3 %multiply_reduce_fusion.1 = (f32[4]{0:T(128)S(1)}, f32[4]{0:T(128)S(1)}, f32[4,2,4,1024]{3,2,1,0:T(4,128)S(1)}) fusion(f32[4,2,4,1024]{3,2,1,0:T(4,128)} %fusion.6, f32[2,4,1024,4]{2,3,1,0:T(4,128)S(1)} %fusion.1, bf16[4,2,512,1024]{3,2,1,0:T(8,128)(2,1)} %param.5, f32[4,512]{1,0:T(4,128)S(1)} %copy-done.2), kind=kOutput, calls=%fused_computation.8 | convolution fusion | flops 67338240 | bytes 8790048 | tf_op jit(solution)/shard_map/fmbs,fmkb->fmks/dot_general | solution.py:51
  211.2 76.0 %all-reduce.1 = (f32[4]{0:T(128)S(1)}, f32[4]{0:T(128)S(1)}) all-reduce(f32[4]{0:T(128)S(1)} %get-tuple-element.4, f32[4]{0:T(128)S(1)} %get-tuple-element.3), channel_id=1, replica_groups=mesh['ma'=32,'freq'=8] {'ma','freq'}, use_global_device_ids=true, to_apply=%region_2.3 | all-reduce | flops 8 | bytes 64 | tf_op jit(solution)/shard_map/psum | solution.py:61
  287.2 0.0 copy-done.1
  287.2 0.9 multiply_reduce_fusion
  288.1 0.0 copy-start.3
  288.1 74.3 %psum.23 = f32[4]{0:T(128)S(1)} all-reduce(f32[4]{0:T(128)S(1)} %get-tuple-element.7), channel_id=1, replica_groups=mesh['ma'=32,'freq'=8] {'ma','freq'}, use_global_device_ids=true, to_apply=%region_6.7 | all-reduce | flops 4 | bytes 32 | tf_op jit(solution)/shard_map/psum | solution.py:65
  362.4 0.8 multiply_add_fusion
  363.1 0.0 copy-done.3
  (3 shorter events, 0.0 us)
Async XLA Ops:
  7.2 192.2 %copy-start = (f32[4,32]{1,0:T(4,128)S(1)}, f32[4,32]{1,0:T(4,128)}, u32[]{:S(2)}) copy-start(f32[4,32]{1,0:T(4,128)} %param.7) | copy-start | bytes 1540
  7.2 194.6 %copy-start.2 = (f32[4,512]{1,0:T(4,128)S(1)}, f32[4,512]{1,0:T(4,128)}, u32[]{:S(2)}) copy-start(f32[4,512]{1,0:T(4,128)} %param.6) | copy-start | bytes 24580
  7.2 158.1 %all-reduce.4.cloned.1.call-start = ((), (), s32[]{:S(2)}) async-start(), calls=%async_computation.1 | async-start | bytes 4194304
  10.3 189.1 %all-gather.2.cloned.1.call-start = ((), (), s32[]{:S(2)}) async-start(), calls=%async_computation | async-start | bytes 1179648 | tf_op jit(solution)/shard_map/all_gather | solution.py:55
  201.8 85.4 %copy-start.1 = (f32[4,2,4,1024]{3,2,1,0:T(4,128)S(1)}, f32[4,2,4,1024]{3,2,1,0:T(4,128)}, u32[]{:S(2)}) copy-start(f32[4,2,4,1024]{3,2,1,0:T(4,128)} %fusion.6) | copy-start | bytes 393220
  288.1 75.0 %copy-start.3 = (f32[4,2,4,1024]{3,2,1,0:T(4,128)}, f32[4,2,4,1024]{3,2,1,0:T(4,128)S(1)}, u32[]{:S(2)}) copy-start(f32[4,2,4,1024]{3,2,1,0:T(4,128)S(1)} %get-tuple-element.8) | copy-start | bytes 393220
Sparse Core Ops, SparseCore 0:
  11.5 153.6 all-reduce.3
  171.7 27.6 all-gather.1
where the time goes:
time: 370 us
  waiting for transfers between devices  181 us (49%)
  blocking collectives  150 us (41%)
  matrix products  18.9 us (5%)
  between operations  14.8 us (4%)
    unnamed x3, waiting for transfers between devices  153 us
    psum x1, blocking collectives, local(): norm_now = lax.psum(local_norm, ('ma', 'freq'))  76 us
    psum x1, blocking collectives, local(): lax.psum(jnp.sum(residual * residual, axis=(0, 1, 3)), ('ma', 'freq'))  74.3 us
    all_gather x1, waiting for transfers between devices, local(): lax.all_gather(right_side, 'freq', axis=0, tiled=True)  27.8 us
    dot_general x1, matrix products, local(): jnp.einsum('fmbs,fmkb->fmks', transfer, scaled, preferred_element_type=jn...  9.35 us
  transfers between devices with their start and end apart: 2, of which 2 were waited for; matrix products, arithmetic and copies ran while one was open for 0% of the time, Pallas kernels for 0%

commit v1 on v0

--- a/solution.py
+++ b/solution.py
@@ -62,7 +62,7 @@
     curvature = lax.psum(local_curve, ("ma", "freq"))
     step_plain = norm_now / curvature
     residual = right_side - step_plain[None, None, :, None] * applied
-    norm_next = lax.psum(jnp.sum(residual * residual, axis=(0, 1, 3)), ("ma", "freq"))
+    norm_next = lax.psum(lax.psum(jnp.sum(residual * residual, axis=(0, 1, 3)), "ma"), "freq")
     sky_map = step_plain[None, None, :, None] * right_side
     direction = residual + (norm_next / norm_now)[None, None, :, None] * right_side
     return (sky_map, residual, direction)

time: 370 us -> 382 us (1.032)
  blocking collectives: 150 us -> 162 us
    psum x1 -> x2, blocking collectives: 74.3 us -> 85.8 us  [the longest x1 59.2 us: local(): lax.psum(jnp.sum(residual * residual, axis=(0, 1, 3)), 'ma')]
where the time goes in v1:
time: 382 us
  waiting for transfers between devices  181 us (47%)
  blocking collectives  162 us (42%)
  matrix products  18.9 us (5%)
  between operations  14.8 us (4%)
    unnamed x3, waiting for transfers between devices  153 us
    psum x1, blocking collectives, local(): norm_now = lax.psum(local_norm, ('ma', 'freq'))  76 us
    psum x1, blocking collectives, local(): lax.psum(jnp.sum(residual * residual, axis=(0, 1, 3)), 'ma')  59.2 us
    all_gather x1, waiting for transfers between devices, local(): lax.all_gather(right_side, 'freq', axis=0, tiled=True)  27.8 us
    psum x1, blocking collectives, local(): lax.psum(lax.psum(jnp.sum(residual * residual, axis=(0, 1, 3)), 'ma'), 'f...  26.6 us
    dot_general x1, matrix products, local(): jnp.einsum('fmbs,fmkb->fmks', transfer, scaled, preferred_element_type=jn...  9.37 us
  transfers between devices with their start and end apart: 2, of which 2 were waited for; matrix products, arithmetic and copies ran while one was open for 0% of the time, Pallas kernels for 0%

profile of v1, /device:TPU:1, one launch (start us, length us, event | category | flops | bytes accessed | tf_op | source)
XLA Modules:
  0.0 381.5 jit_solution(15595548547362911668)
XLA Ops:
  7.2 0.0 copy-start
  7.2 0.0 copy-start.2
  7.2 0.0 all-reduce.4.cloned.1.call-start
  7.2 1.1 reshape.20
  8.4 1.9 fusion.16
  10.3 0.0 all-reduce.4.cloned.1.call-update
  10.3 0.0 all-gather.2.cloned.1.call-start
  10.3 1.3 dynamic-slice
  12.3 153.0 %all-reduce.4.cloned.1.call-done = f32[64,8192]{1,0:T(8,128)} async-done(((f32[64,8192]{1,0:T(8,128)}), f32[64,8192]{1,0:T(8,128)}) %all-reduce.4.cloned.1.call-update) | async-done | bytes 2097168
  165.3 1.0 constant_dynamic-slice_fusion
  166.3 0.1 reshape.21
  166.3 5.3 %fusion.6 = f32[4,2,4,1024]{3,2,1,0:T(4,128)} fusion(bf16[4,2,512,1024]{3,2,1,0:T(8,128)(2,1)} %param.5, f32[2,4,4,512]{3,2,1,0:T(4,128)S(1)} %reshape.21, f32[4,512]{1,0:T(4,128)} %param.6), kind=kOutput, calls=%fused_computation.14 | convolution fusion | flops 33587200 | bytes 8593408 | tf_op jit(solution)/shard_map/fmbs,mfkb->fmks/dot_general | solution.py:43
  171.6 0.0 all-gather.2.cloned.1.call-update
  171.6 27.8 %all-gather.2.cloned.1.call-done = f32[32,2,4,1024]{3,2,1,0:T(4,128)} async-done(((f32[4,2,4,1024]{3,2,1,0:T(4,128)}), f32[32,2,4,1024]{3,2,1,0:T(4,128)}) %all-gather.2.cloned.1.call-update) | async-done | bytes 1048592 | tf_op jit(solution)/shard_map/all_gather | solution.py:55
  199.4 0.0 copy-done
  199.4 2.4 fusion.1
  201.8 0.0 copy-done.2
  201.8 0.0 copy-start.1
  201.8 9.4 %multiply_reduce_fusion.1 = (f32[4]{0:T(128)S(1)}, f32[4]{0:T(128)S(1)}, f32[4,2,4,1024]{3,2,1,0:T(4,128)S(1)}) fusion(f32[4,2,4,1024]{3,2,1,0:T(4,128)} %fusion.6, f32[2,4,1024,4]{2,3,1,0:T(4,128)S(1)} %fusion.1, bf16[4,2,512,1024]{3,2,1,0:T(8,128)(2,1)} %param.5, f32[4,512]{1,0:T(4,128)S(1)} %copy-done.2), kind=kOutput, calls=%fused_computation.8 | convolution fusion | flops 67338240 | bytes 8790048 | tf_op jit(solution)/shard_map/fmbs,fmkb->fmks/dot_general | solution.py:51
  211.2 76.0 %all-reduce.1 = (f32[4]{0:T(128)S(1)}, f32[4]{0:T(128)S(1)}) all-reduce(f32[4]{0:T(128)S(1)} %get-tuple-element.4, f32[4]{0:T(128)S(1)} %get-tuple-element.3), channel_id=1, replica_groups=mesh['ma'=32,'freq'=8] {'ma','freq'}, use_global_device_ids=true, to_apply=%region_2.3 | all-reduce | flops 8 | bytes 64 | tf_op jit(solution)/shard_map/psum | solution.py:61
  287.2 0.0 copy-done.1
  287.2 0.9 multiply_reduce_fusion
  288.1 0.0 copy-start.3
  288.1 59.2 %psum.30 = f32[4]{0:T(128)S(1)} all-reduce(f32[4]{0:T(128)S(1)} %get-tuple-element.7), channel_id=1, replica_groups=mesh['ma'=32,'freq'=8] {'ma'}, use_global_device_ids=true, to_apply=%region_6.7 | all-reduce | flops 4 | bytes 32 | tf_op jit(solution)/shard_map/psum | solution.py:65
  347.3 26.6 %psum.31 = f32[4]{0:T(128)S(1)} all-reduce(f32[4]{0:T(128)S(1)} %psum.30), channel_id=1, replica_groups=mesh['ma'=32,'freq'=8] {'freq'}, use_global_device_ids=true, to_apply=%region_7.8 | all-reduce | flops 4 | bytes 32 | tf_op jit(solution)/shard_map/psum | solution.py:65
  373.9 0.8 multiply_add_fusion
  374.7 0.0 copy-done.3
  (3 shorter events, 0.0 us)
Async XLA Ops:
  7.2 192.2 %copy-start = (f32[4,32]{1,0:T(4,128)S(1)}, f32[4,32]{1,0:T(4,128)}, u32[]{:S(2)}) copy-start(f32[4,32]{1,0:T(4,128)} %param.7) | copy-start | bytes 1540
  7.2 194.6 %copy-start.2 = (f32[4,512]{1,0:T(4,128)S(1)}, f32[4,512]{1,0:T(4,128)}, u32[]{:S(2)}) copy-start(f32[4,512]{1,0:T(4,128)} %param.6) | copy-start | bytes 24580
  7.2 158.1 %all-reduce.4.cloned.1.call-start = ((), (), s32[]{:S(2)}) async-start(), calls=%async_computation.1 | async-start | bytes 4194304
  10.3 189.1 %all-gather.2.cloned.1.call-start = ((), (), s32[]{:S(2)}) async-start(), calls=%async_computation | async-start | bytes 1179648 | tf_op jit(solution)/shard_map/all_gather | solution.py:55
  201.8 85.4 %copy-start.1 = (f32[4,2,4,1024]{3,2,1,0:T(4,128)S(1)}, f32[4,2,4,1024]{3,2,1,0:T(4,128)}, u32[]{:S(2)}) copy-start(f32[4,2,4,1024]{3,2,1,0:T(4,128)} %fusion.6) | copy-start | bytes 393220
  288.1 86.6 %copy-start.3 = (f32[4,2,4,1024]{3,2,1,0:T(4,128)}, f32[4,2,4,1024]{3,2,1,0:T(4,128)S(1)}, u32[]{:S(2)}) copy-start(f32[4,2,4,1024]{3,2,1,0:T(4,128)S(1)} %get-tuple-element.8) | copy-start | bytes 393220
Sparse Core Ops, SparseCore 0:
  11.5 153.6 all-reduce.3
  171.7 27.6 all-gather.1
